TPU v7x, 512 devices: a whole 4x4x16 slice. The times are simulated.
512 devices in a mesh: leaf: 32 (over x, y, core), front: 16 (over z).
Axes of the slice: x: 4, y: 4, z: 16, core: 2. Of those that a mesh axis runs over, the one named last changes fastest.
Arguments:
- panel_0: float32 [2, 1024, 1024], P(None, 'front', 'leaf'), as said below
- panel_1: float32 [2, 1024, 2048], P(None, 'front', 'leaf'), as said below
- panel_2: float32 [2, 1024, 4096], P(None, 'front', 'leaf'), as said below
- panel_3: float32 [2, 1024, 8192], P(None, 'front', 'leaf'), as said below
- load_0: float32 [1024, 128], P('leaf'), may hold values from -6 to 6
- load_1: float32 [2048, 128], P('leaf'), may hold values from -6 to 6
- load_2: float32 [4096, 128], P('leaf'), may hold values from -6 to 6
- load_3: float32 [8192, 128], P('leaf'), may hold values from -6 to 6
- inflow: float32 [8, 1024, 128], P(None, 'front'), may hold values from -6 to 6
- above_solution: float32 [1024, 128], replicated, may hold values from -6 to 6
- block_maps: int32 [14, 16], replicated, may hold values from 0 to 31, as said below
Outputs:
- solution_0: float32 [1024, 128], P(('leaf', 'front'))
- solution_1: float32 [2048, 128], P(('leaf', 'front'))
- solution_2: float32 [4096, 128], P(('leaf', 'front'))
- solution_3: float32 [8192, 128], P(('leaf', 'front'))
- top_update: float32 [1024, 128], P('front')
Inputs may be any that keep to these rules, and one draw needn't show every extreme that they name: `block_maps`: the 16 entries of each row are distinct. `panel_0`: within each front the pivot block K is lower triangular with diagonal entries of 0.8 to 1.25. `panel_1`: within each front the pivot block K is lower triangular with diagonal entries of 0.8 to 1.25. `panel_2`: within each front the pivot block K is lower triangular with diagonal entries of 0.8 to 1.25. `panel_3`: within each front the pivot block K is lower triangular with diagonal entries of 0.8 to 1.25.
All inputs are finite; a program needn't handle non-finite values.
Results may differ from a plain program's by a relative error of at most 0.00013.
Values sent between devices are 32-bit elements; how exact they have to be, the bound alone decides.
No kernel may reach another device: no remote copies, remote signals or barrier semaphores. Data moves between devices by JAX's collectives and lax.ppermute only.
A program may use at most 64 MiB of HBM per device.

v0:
```python
import jax
import jax.numpy as jnp
from jax import lax
from jax.sharding import PartitionSpec as P

exact_precision = lax.Precision.HIGHEST


def partner_2(value, axis, distance):
    mask = 2**distance
    pairs = [(source, source ^ mask) for source in range(lax.axis_size(axis))]
    return lax.ppermute(value, axis, pairs)


def group_total(partial_sum, group_bits, level_id):
    leaf_pos = lax.axis_index("leaf")
    group_count = 1 << level_id
    slot_id = leaf_pos >> group_bits
    chosen = (jnp.arange(group_count, dtype=jnp.int32) == slot_id).astype(jnp.float32)
    spread_out = chosen.reshape((group_count,) + (1,) * partial_sum.ndim) * partial_sum[None]
    totals = lax.psum(spread_out, "leaf")
    return lax.dynamic_index_in_dim(totals, slot_id, 0, keepdims=False)


def group_concat(column_block, group_bits):
    leaf_pos = lax.axis_index("leaf")
    for section_bit in range(group_bits):
        partner = partner_2(column_block, "leaf", section_bit)
        upper_half = leaf_pos >> section_bit & 1 == 1
        column_block = jnp.where(
            upper_half,
            jnp.concatenate([partner, column_block], 0),
            jnp.concatenate([column_block, partner], 0),
        )
    return column_block


def place_blocks(map_row, values, block_rows):
    block_count = map_row.shape[0]
    targets = jnp.arange(2 * block_count, dtype=jnp.int32)
    selector_matrix = (targets[:, None] == map_row[None, :]).astype(jnp.float32)
    factor_blocks = values.reshape(block_count, block_rows, values.shape[1])
    return jnp.einsum("du,uye->dye", selector_matrix, factor_blocks, precision=exact_precision)


def lift_update(update_block, level_id, group_bits, block_maps, sep_rows):
    leaf_pos = lax.axis_index("leaf")
    front_pos = lax.axis_index("front")
    block_rows = update_block.shape[0]
    block_count = sep_rows // block_rows
    group_size = 1 << group_bits
    child_id = leaf_pos >> group_bits
    base_row = (1 << level_id) - 2
    own_map = lax.dynamic_index_in_dim(block_maps, base_row + child_id, 0, keepdims=False)
    parent_pos = leaf_pos % (2 * group_size)
    parent_rows = sep_rows // (2 * group_size)
    other_map = lax.dynamic_index_in_dim(block_maps, base_row + (child_id ^ 1), 0, keepdims=False)
    partner_block = partner_2(update_block, "leaf", group_bits)
    own_full, other_full = (
        lax.all_gather(update_block, "front", axis=0, tiled=True),
        lax.all_gather(partner_block, "front", axis=0, tiled=True),
    )
    placed = place_blocks(own_map, own_full, block_rows) + place_blocks(
        other_map, other_full, block_rows
    )
    separator = placed[:block_count].reshape(sep_rows, -1)
    sep_part = lax.dynamic_slice_in_dim(separator, parent_pos * parent_rows, parent_rows, 0)
    border = lax.dynamic_index_in_dim(placed, block_count + front_pos, 0, keepdims=False)
    return (sep_part, border)


def on_device(
    panel_0,
    panel_1,
    panel_2,
    panel_3,
    load_0,
    load_1,
    load_2,
    load_3,
    inflow,
    above_solution,
    block_maps,
):
    panels = (panel_0, panel_1, panel_2, panel_3)
    load_list = (load_0, load_1, load_2, load_3)
    level_count = len(panels)
    leaf_pos = lax.axis_index("leaf")
    front_pos = lax.axis_index("front")
    front_count = lax.axis_size("front")
    total_bits = lax.axis_size("leaf").bit_length() - 1
    block_rows = panel_0.shape[1]
    sep_rows = block_rows * front_count
    solved = [None] * level_count
    lifted = None
    top_block = None
    for level_id in range(level_count - 1, -1, -1):
        group_bits = total_bits - level_id
        right_side = load_list[level_id]
        if level_id == level_count - 1:
            front_id = leaf_pos >> group_bits
            border = lax.dynamic_index_in_dim(inflow, front_id, 0, keepdims=False)
        else:
            right_side = right_side + lifted[0]
            border = lifted[1]
        partial_sum = jnp.einsum(
            "ksc,cr->ksr", panels[level_id], right_side, precision=exact_precision
        )
        totals = group_total(partial_sum, group_bits, level_id)
        solved[level_id] = totals[0]
        update_block = border - totals[1]
        if level_id > 0:
            lifted = lift_update(update_block, level_id, group_bits, block_maps, sep_rows)
        else:
            top_block = update_block
    upper_full = above_solution
    upper_block = lax.dynamic_slice_in_dim(above_solution, front_pos * block_rows, block_rows, 0)
    targets = jnp.arange(2 * front_count, dtype=jnp.int32)
    pieces = []
    for level_id in range(level_count):
        group_bits = total_bits - level_id
        stacked = jnp.stack([solved[level_id], -upper_block])
        partial_sum = jnp.einsum(
            "ksc,ksr->cr", panels[level_id], stacked, precision=exact_precision
        )
        column_block = lax.psum(partial_sum, "front")
        span_rows = column_block.shape[0] // front_count
        pieces.append(lax.dynamic_slice_in_dim(column_block, front_pos * span_rows, span_rows, 0))
        if level_id < level_count - 1:
            full_solution = group_concat(column_block, group_bits)
            ancestor_blocks = jnp.concatenate([full_solution, upper_full], 0).reshape(
                2 * front_count, block_rows, -1
            )
            child_id = leaf_pos >> group_bits - 1
            child_map = lax.dynamic_index_in_dim(
                block_maps, (2 << level_id) - 2 + child_id, 0, keepdims=False
            )
            selector_matrix = (child_map[:, None] == targets[None, :]).astype(jnp.float32)
            upper_factor_blocks = jnp.einsum(
                "gq,qzk->gzk", selector_matrix, ancestor_blocks, precision=exact_precision
            )
            upper_full = upper_factor_blocks.reshape(sep_rows, -1)
            upper_block = lax.dynamic_index_in_dim(
                upper_factor_blocks, front_pos, 0, keepdims=False
            )
    return (pieces[0], pieces[1], pieces[2], pieces[3], top_block)


def solution(mesh):
    in_specs = (
        P(None, "front", "leaf"),
        P(None, "front", "leaf"),
        P(None, "front", "leaf"),
        P(None, "front", "leaf"),
        P("leaf", None),
        P("leaf", None),
        P("leaf", None),
        P("leaf", None),
        P(None, "front", None),
        P(),
        P(),
    )
    out_specs = (
        P(("leaf", "front"), None),
        P(("leaf", "front"), None),
        P(("leaf", "front"), None),
        P(("leaf", "front"), None),
        P("front", None),
    )
    return jax.shard_map(
        on_device, mesh=mesh, in_specs=in_specs, out_specs=out_specs, check_vma=False
    )
```

profile of v0, /device:TPU:2, one launch (start us, length us, event | category | flops | bytes accessed | tf_op | source)
XLA Modules:
  0.0 1208.8 jit_solution(1407500976551751530)
XLA Ops:
  7.2 0.8 copy-done
  8.1 1.2 fusion.16
  9.3 0.9 broadcast_multiply_fusion
  10.3 0.9 fusion.74
  11.1 138.3 %all-reduce.7.cloned.1.call-done = f32[8,2,64,128]{3,2,1,0:T(8,128)} async-done(((f32[8,2,64,128]{3,2,1,0:T(8,128)}), f32[8,2,64,128]{3,2,1,0:T(8,128)}) %all-reduce.7.cloned.1.call-update) | async-done | bytes 524304 | tf_op jit(solution)/shard_map/psum | solution.py:21
  149.4 0.8 fusion.32
  150.2 4.2 collective-permute-start
  154.4 33.1 %all_gather.18 = f32[1024,128]{1,0:T(8,128)S(1)} all-gather(f32[64,128]{1,0:T(8,128)S(1)} %fusion.32), channel_id=1, replica_groups=mesh['leaf'=32,'front'=16] {'front'}, dimensions={0}, use_global_device_ids=true | all-gather | bytes 557056 | tf_op jit(solution)/shard_map/all_gather | solution.py:60
  187.6 0.9 fusion.14
  188.5 30.6 %all_gather.19 = f32[1024,128]{1,0:T(8,128)S(1)} all-gather(f32[64,128]{1,0:T(8,128)S(1)} %collective-permute-done), channel_id=1, replica_groups=mesh['leaf'=32,'front'=16] {'front'}, dimensions={0}, use_global_device_ids=true | all-gather | bytes 557056 | tf_op jit(solution)/shard_map/all_gather | solution.py:61
  219.1 1.0 convolution_add_fusion.2
  221.2 0.8 broadcast_multiply_fusion.1
  222.2 127.9 %all-reduce.9.cloned.1.call-done = f32[4,2,64,128]{3,2,1,0:T(8,128)} async-done(((f32[4,2,64,128]{3,2,1,0:T(8,128)}), f32[4,2,64,128]{3,2,1,0:T(8,128)}) %all-reduce.9.cloned.1.call-update) | async-done | bytes 262160 | tf_op jit(solution)/shard_map/psum | solution.py:21
  350.8 3.0 collective-permute-start.1
  353.8 33.6 %all_gather.20 = f32[1024,128]{1,0:T(8,128)S(1)} all-gather(f32[64,128]{1,0:T(8,128)S(1)} %fusion.31), channel_id=1, replica_groups=mesh['leaf'=32,'front'=16] {'front'}, dimensions={0}, use_global_device_ids=true | all-gather | bytes 557056 | tf_op jit(solution)/shard_map/all_gather | solution.py:60
  387.4 0.9 fusion.11
  388.3 30.1 %all_gather.21 = f32[1024,128]{1,0:T(8,128)S(1)} all-gather(f32[64,128]{1,0:T(8,128)S(1)} %collective-permute-done.1), channel_id=1, replica_groups=mesh['leaf'=32,'front'=16] {'front'}, dimensions={0}, use_global_device_ids=true | all-gather | bytes 557056 | tf_op jit(solution)/shard_map/all_gather | solution.py:61
  418.4 1.0 convolution_add_fusion.1
  421.3 126.1 %all-reduce.11.cloned.1.call-done = f32[2,2,64,128]{3,2,1,0:T(8,128)} async-done(((f32[2,2,64,128]{3,2,1,0:T(8,128)}), f32[2,2,64,128]{3,2,1,0:T(8,128)}) %all-reduce.11.cloned.1.call-update) | async-done | bytes 131088 | tf_op jit(solution)/shard_map/psum | solution.py:21
  548.2 5.2 collective-permute-start.2
  553.4 33.3 %all_gather.22 = f32[1024,128]{1,0:T(8,128)S(1)} all-gather(f32[64,128]{1,0:T(8,128)S(1)} %fusion.30), channel_id=1, replica_groups=mesh['leaf'=32,'front'=16] {'front'}, dimensions={0}, use_global_device_ids=true | all-gather | bytes 557056 | tf_op jit(solution)/shard_map/all_gather | solution.py:60
  586.7 0.9 fusion.8
  587.6 30.3 %all_gather.23 = f32[1024,128]{1,0:T(8,128)S(1)} all-gather(f32[64,128]{1,0:T(8,128)S(1)} %collective-permute-done.2), channel_id=1, replica_groups=mesh['leaf'=32,'front'=16] {'front'}, dimensions={0}, use_global_device_ids=true | all-gather | bytes 557056 | tf_op jit(solution)/shard_map/all_gather | solution.py:61
  617.9 1.0 convolution_add_fusion
  619.7 0.9 fusion
  620.7 120.9 %all-reduce.13.cloned.1.call-done = f32[1,2,64,128]{3,2,1,0:T(8,128)} async-done(((f32[1,2,64,128]{3,2,1,0:T(8,128)}), f32[1,2,64,128]{3,2,1,0:T(8,128)}) %all-reduce.13.cloned.1.call-update) | async-done | bytes 65552 | tf_op jit(solution)/shard_map/psum | solution.py:21
  742.6 56.8 %psum.60 = f32[32,128]{1,0:T(8,128)S(1)} all-reduce(f32[32,128]{1,0:T(8,128)S(1)} %convolution_bitcast_fusion.5), channel_id=1, replica_groups=mesh['leaf'=32,'front'=16] {'front'}, use_global_device_ids=true, to_apply=%region_4.5 | all-reduce | flops 4096 | bytes 32768 | tf_op jit(solution)/shard_map/psum | solution.py:126
  799.4 1.9 collective-permute-start.3
  801.3 1.1 collective-permute-done.3
  802.4 3.4 collective-permute-start.4
  805.8 2.4 collective-permute-done.4
  808.2 4.6 collective-permute-start.5
  812.8 3.1 collective-permute-done.5
  815.9 3.3 collective-permute-start.6
  819.3 3.5 collective-permute-done.6
  822.8 4.1 collective-permute-start.7
  826.9 0.8 constant_dynamic-slice_fusion.7
  827.6 4.9 collective-permute-done.7
  832.7 1.1 fusion.5
  834.2 53.5 %psum.61 = f32[64,128]{1,0:T(8,128)S(1)} all-reduce(f32[64,128]{1,0:T(8,128)S(1)} %convolution_bitcast_fusion.4), channel_id=1, replica_groups=mesh['leaf'=32,'front'=16] {'front'}, use_global_device_ids=true, to_apply=%region_5.6 | all-reduce | flops 8192 | bytes 65536 | tf_op jit(solution)/shard_map/psum | solution.py:126
  887.7 1.9 collective-permute-start.8
  889.6 1.2 collective-permute-done.8
  890.8 3.4 collective-permute-start.9
  894.1 2.8 collective-permute-done.9
  896.9 4.6 collective-permute-start.10
  901.5 3.8 collective-permute-done.10
  905.3 3.5 collective-permute-start.11
  908.9 0.8 constant_dynamic-slice_fusion.10
  909.8 3.8 collective-permute-done.11
  913.7 1.1 fusion.3
  914.9 0.9 convolution_bitcast_fusion.1
  915.9 129.0 %all-reduce.15.cloned.1.call-done = f32[128,128]{0,1:T(8,128)} async-done(((f32[128,128]{0,1:T(8,128)}), f32[128,128]{0,1:T(8,128)}) %all-reduce.15.cloned.1.call-update) | async-done | bytes 65552 | tf_op jit(solution)/shard_map/psum | solution.py:126
  1044.9 1.9 collective-permute-start.12
  1046.8 1.4 collective-permute-done.12
  1048.2 0.9 maximum_select_fusion.8
  1049.1 3.4 collective-permute-start.13
  1052.5 0.8 dynamic-slice_bitcast_fusion
  1053.4 3.2 collective-permute-done.13
  1056.6 4.9 collective-permute-start.14
  1063.1 4.4 collective-permute-done.14
  1068.0 1.1 fusion.1
  1069.2 1.0 convolution_bitcast_fusion
  1071.7 128.7 %all-reduce.17.cloned.1.call-done = f32[256,128]{0,1:T(8,128)} async-done(((f32[256,128]{0,1:T(8,128)}), f32[256,128]{0,1:T(8,128)}) %all-reduce.17.cloned.1.call-update) | async-done | bytes 131088 | tf_op jit(solution)/shard_map/psum | solution.py:126
  1200.4 0.9 constant_dynamic-slice_fusion.1
  (85 shorter events, 11.9 us)
Async XLA Ops:
  7.2 0.9 copy-start
  7.2 142.3 %all-reduce.7.cloned.1.call-start = ((), (), s32[]{:S(2)}) async-start(), calls=%async_computation | async-start | bytes 1048576 | tf_op jit(solution)/shard_map/psum | solution.py:21
  10.2 339.9 %all-reduce.9.cloned.1.call-start = ((), (), s32[]{:S(2)}) async-start(), calls=%async_computation.1 | async-start | bytes 524288 | tf_op jit(solution)/shard_map/psum | solution.py:21
  150.2 38.2 %collective-permute-start = (f32[64,128]{1,0:T(8,128)S(1)}, f32[64,128]{1,0:T(8,128)S(1)}, u32[]{:S(2)}, u32[]{:S(2)}) collective-permute-start(f32[64,128]{1,0:T(8,128)S(1)} %fusion.32), channel_id=1, source_target_pairs={{0,64},{16,80},{32,96},{48,112},{64,0},{80,16},{96,32},{112,48},{1... | collective-permute-start | bytes 98312 | tf_op jit(solution)/shard_map/ppermute | solution.py:12
  220.1 0.8 copy-start.3
  220.1 0.9 copy-start.7
  222.0 325.4 %all-reduce.11.cloned.1.call-start = ((), (), s32[]{:S(2)}) async-start(), calls=%async_computation.2 | async-start | bytes 262144 | tf_op jit(solution)/shard_map/psum | solution.py:21
  350.8 37.5 %collective-permute-start.1 = (f32[64,128]{1,0:T(8,128)S(1)}, f32[64,128]{1,0:T(8,128)S(1)}, u32[]{:S(2)}, u32[]{:S(2)}) collective-permute-start(f32[64,128]{1,0:T(8,128)S(1)} %fusion.31), channel_id=1, source_target_pairs={{0,128},{16,144},{32,160},{48,176},{64,192},{80,208},{96,224},{112... | collective-permute-start | bytes 98312 | tf_op jit(solution)/shard_map/ppermute | solution.py:12
  419.4 0.8 copy-start.2
  419.5 0.8 copy-start.8
  421.2 320.4 %all-reduce.13.cloned.1.call-start = ((), (), s32[]{:S(2)}) async-start(), calls=%async_computation.3 | async-start | bytes 131072 | tf_op jit(solution)/shard_map/psum | solution.py:21
  548.2 39.5 %collective-permute-start.2 = (f32[64,128]{1,0:T(8,128)S(1)}, f32[64,128]{1,0:T(8,128)S(1)}, u32[]{:S(2)}, u32[]{:S(2)}) collective-permute-start(f32[64,128]{1,0:T(8,128)S(1)} %fusion.30), channel_id=1, source_target_pairs={{0,256},{16,272},{32,288},{48,304},{64,320},{80,336},{96,352},{112... | collective-permute-start | bytes 98312 | tf_op jit(solution)/shard_map/ppermute | solution.py:12
  618.9 0.8 copy-start.5
  619.0 0.8 copy-start.9
  619.0 1.7 copy-start.1
  620.7 424.2 %all-reduce.15.cloned.1.call-start = ((), (), s32[]{:S(2)}) async-start(), calls=%async_computation.4 | async-start | bytes 131072 | tf_op jit(solution)/shard_map/psum | solution.py:126
  799.4 3.1 collective-permute-start.3
  802.4 5.8 collective-permute-start.4
  808.2 7.7 collective-permute-start.5
  815.9 6.9 collective-permute-start.6
  822.8 9.8 collective-permute-start.7
  887.7 3.1 collective-permute-start.8
  890.8 6.2 collective-permute-start.9
  896.9 8.4 collective-permute-start.10
  905.3 8.3 collective-permute-start.11
  915.9 284.5 %all-reduce.17.cloned.1.call-start = ((), (), s32[]{:S(2)}) async-start(), calls=%async_computation.5 | async-start | bytes 262144 | tf_op jit(solution)/shard_map/psum | solution.py:126
  1044.9 3.3 collective-permute-start.12
  1049.1 7.5 collective-permute-start.13
  1053.4 8.8 copy-start.6
  1056.6 10.9 collective-permute-start.14
  1070.1 0.8 copy-start.4
Sparse Core Ops, SparseCore 0:
  11.2 138.1 all-reduce.6
  222.1 127.8 all-reduce.8
  421.4 126.0 all-reduce.10
  620.8 120.7 all-reduce.12
  916.0 128.8 all-reduce.14
  1070.3 130.0 all-reduce.16
where the time goes:
time: 1210 us
  waiting for transfers between devices  806 us (67%)
  blocking collectives  301 us (25%)
  starting transfers between devices  53.6 us (4%)
  between operations  14.8 us (1%)
  matrix products  13.7 us (1%)
    psum x4, waiting for transfers between devices, group_total(): totals = lax.psum(spread_out, 'leaf')  513 us
    psum x2, waiting for transfers between devices, on_device(): column_block = lax.psum(partial_sum, 'front')  258 us
    psum x2, blocking collectives, on_device(): column_block = lax.psum(partial_sum, 'front')  110 us
    all_gather x3, blocking collectives, lift_update(): lax.all_gather(update_block, 'front', axis=0, tiled=True)  100 us
    all_gather x3, blocking collectives, lift_update(): lax.all_gather(partner_block, 'front', axis=0, tiled=True)  91 us
    ppermute x15, starting transfers between devices, partner_2(): return lax.ppermute(value, axis, pairs)  53.4 us
    ppermute x15, waiting for transfers between devices, partner_2(): return lax.ppermute(value, axis, pairs)  35.6 us
  transfers between devices with their start and end apart: 21, of which 18 were waited for; matrix products, arithmetic and copies ran while one was open for 1% of the time, Pallas kernels for 0%

commit v1 on v0

--- a/solution.py
+++ b/solution.py
@@ -4,6 +4,19 @@
 from jax.sharding import PartitionSpec as P
 
 exact_precision = lax.Precision.HIGHEST
+
+
+def collect(x, axis, dim):
+    ways = lax.axis_size(axis)
+    up = [(d, (d + 1) % ways) for d in range(ways)]
+    down = [(d, (d - 1) % ways) for d in range(ways)]
+    earlier, later = ([x], [x])
+    for _ in range(ways // 2):
+        earlier.append(lax.ppermute(earlier[-1], axis, up))
+    for _ in range((ways - 1) // 2):
+        later.append(lax.ppermute(later[-1], axis, down))
+    line = jnp.concatenate([*earlier[::-1], *later[1:]], axis=dim)
+    return jnp.roll(line, (lax.axis_index(axis) - ways // 2) * x.shape[dim], axis=dim)
 
 
 def partner_2(value, axis, distance):
@@ -58,7 +71,7 @@
     partner_block = partner_2(update_block, "leaf", group_bits)
     own_full, other_full = (
         lax.all_gather(update_block, "front", axis=0, tiled=True),
-        lax.all_gather(partner_block, "front", axis=0, tiled=True),
+        collect(partner_block, "front", 0),
     )
     placed = place_blocks(own_map, own_full, block_rows) + place_blocks(
         other_map, other_full, block_rows

time: 1210 us -> 1310 us (1.083)
  starting transfers between devices: 53.6 us -> 202 us
  blocking collectives: 301 us -> 210 us
  waiting for transfers between devices: 806 us -> 842 us
    ppermute x0 -> x45, starting transfers between devices: none -> 149 us  [the longest x21 92.1 us: collect(): later.append(lax.ppermute(later[-1], axis, down))]
    all_gather x3 -> x0, blocking collectives: 91 us -> none  [lift_update(): lax.all_gather(partner_block, 'front', axis=0, tiled=True)]
    ppermute x0 -> x45, waiting for transfers between devices: none -> 20.6 us  [the longest x24 13.2 us: collect(): earlier.append(lax.ppermute(earlier[-1], axis, up))]
  transfers between devices with their start and end apart: 21 -> 66, of which waited for: 18 -> 27; matrix products, arithmetic and copies ran while one was open for 1% -> 1% of each run, Pallas kernels for 0% -> 0%
where the time goes in v1:
time: 1310 us; the launch traced here: 1300 us
  waiting for transfers between devices  842 us (64%)
  blocking collectives  210 us (16%)
  starting transfers between devices  202 us (15%)
  between operations  15.8 us (1%)
  matrix products  13.7 us (1%)
    psum x4, waiting for transfers between devices, group_total(): totals = lax.psum(spread_out, 'leaf')  520 us
    psum x2, waiting for transfers between devices, on_device(): column_block = lax.psum(partial_sum, 'front')  258 us
    psum x2, blocking collectives, on_device(): column_block = lax.psum(partial_sum, 'front')  110 us
    all_gather x3, blocking collectives, lift_update(): lax.all_gather(update_block, 'front', axis=0, tiled=True)  100 us
    ppermute x21, starting transfers between devices, collect(): later.append(lax.ppermute(later[-1], axis, down))  92.1 us
    ppermute x24, starting transfers between devices, collect(): earlier.append(lax.ppermute(earlier[-1], axis, up))  56.6 us
    ppermute x15, starting transfers between devices, partner_2(): return lax.ppermute(value, axis, pairs)  53.2 us
    ppermute x15, waiting for transfers between devices, partner_2(): return lax.ppermute(value, axis, pairs)  43.7 us
  transfers between devices with their start and end apart: 66, of which 27 were waited for; matrix products, arithmetic and copies ran while one was open for 1% of the time, Pallas kernels for 0%

profile of v1, /device:TPU:2, one launch (start us, length us, event | category | flops | bytes accessed | tf_op | source)
XLA Modules:
  0.0 1304.5 jit_solution(1061403018717849188)
XLA Ops:
  10.2 139.2 %all-reduce.7.cloned.1.call-done = f32[8,2,64,128]{3,2,1,0:T(8,128)} async-done(((f32[8,2,64,128]{3,2,1,0:T(8,128)}), f32[8,2,64,128]{3,2,1,0:T(8,128)}) %all-reduce.7.cloned.1.call-update) | async-done | bytes 524304 | tf_op jit(solution)/shard_map/psum | solution.py:34
  150.2 4.2 collective-permute-start
  154.4 3.1 collective-permute-done
  157.5 3.5 collective-permute-start.1
  161.0 4.4 collective-permute-done.1
  167.3 5.1 collective-permute-start.9
  174.4 5.1 collective-permute-start.10
  181.5 5.1 collective-permute-start.11
  189.4 5.1 collective-permute-start.12
  196.6 5.1 collective-permute-start.13
  203.6 33.5 %all_gather.9 = f32[1024,128]{1,0:T(8,128)S(1)} all-gather(f32[64,128]{1,0:T(8,128)S(1)} %fusion.35), channel_id=1, replica_groups=mesh['leaf'=32,'front'=16] {'front'}, dimensions={0}, use_global_device_ids=true | all-gather | bytes 557056 | tf_op jit(solution)/shard_map/all_gather | solution.py:73
  239.1 3.9 collective-permute-start.8
  244.0 3.1 collective-permute-start.15
  247.3 2.5 collective-permute-done.15
  253.1 129.4 %all-reduce.9.cloned.1.call-done = f32[4,2,64,128]{3,2,1,0:T(8,128)} async-done(((f32[4,2,64,128]{3,2,1,0:T(8,128)}), f32[4,2,64,128]{3,2,1,0:T(8,128)}) %all-reduce.9.cloned.1.call-update) | async-done | bytes 262160 | tf_op jit(solution)/shard_map/psum | solution.py:34
  383.2 3.0 collective-permute-start.16
  386.3 2.8 collective-permute-done.16
  389.0 3.4 collective-permute-start.17
  392.5 4.4 collective-permute-done.17
  398.8 5.1 collective-permute-start.25
  405.9 5.1 collective-permute-start.26
  413.0 5.1 collective-permute-start.27
  420.1 5.1 collective-permute-start.28
  427.2 5.1 collective-permute-start.29
  434.3 33.2 %all_gather.10 = f32[1024,128]{1,0:T(8,128)S(1)} all-gather(f32[64,128]{1,0:T(8,128)S(1)} %fusion.34), channel_id=1, replica_groups=mesh['leaf'=32,'front'=16] {'front'}, dimensions={0}, use_global_device_ids=true | all-gather | bytes 557056 | tf_op jit(solution)/shard_map/all_gather | solution.py:73
  469.4 3.9 collective-permute-start.24
  474.2 3.1 collective-permute-start.31
  477.6 2.5 collective-permute-done.31
  483.3 128.1 %all-reduce.11.cloned.1.call-done = f32[2,2,64,128]{3,2,1,0:T(8,128)} async-done(((f32[2,2,64,128]{3,2,1,0:T(8,128)}), f32[2,2,64,128]{3,2,1,0:T(8,128)}) %all-reduce.11.cloned.1.call-update) | async-done | bytes 131088 | tf_op jit(solution)/shard_map/psum | solution.py:34
  612.2 5.2 collective-permute-start.32
  619.5 3.5 collective-permute-start.33
  622.9 4.4 collective-permute-done.33
  629.2 5.1 collective-permute-start.41
  636.3 5.1 collective-permute-start.42
  643.4 5.1 collective-permute-start.43
  650.5 5.1 collective-permute-start.44
  657.6 5.1 collective-permute-start.45
  664.7 33.2 %all_gather.11 = f32[1024,128]{1,0:T(8,128)S(1)} all-gather(f32[64,128]{1,0:T(8,128)S(1)} %fusion.33), channel_id=1, replica_groups=mesh['leaf'=32,'front'=16] {'front'}, dimensions={0}, use_global_device_ids=true | all-gather | bytes 557056 | tf_op jit(solution)/shard_map/all_gather | solution.py:73
  699.8 3.9 collective-permute-start.40
  704.7 3.1 collective-permute-start.47
  708.0 2.5 collective-permute-done.47
  713.8 123.5 %all-reduce.13.cloned.1.call-done = f32[1,2,64,128]{3,2,1,0:T(8,128)} async-done(((f32[1,2,64,128]{3,2,1,0:T(8,128)}), f32[1,2,64,128]{3,2,1,0:T(8,128)}) %all-reduce.13.cloned.1.call-update) | async-done | bytes 65552 | tf_op jit(solution)/shard_map/psum | solution.py:34
  838.3 56.8 %psum.60 = f32[32,128]{1,0:T(8,128)S(1)} all-reduce(f32[32,128]{1,0:T(8,128)S(1)} %convolution_bitcast_fusion.5), channel_id=1, replica_groups=mesh['leaf'=32,'front'=16] {'front'}, use_global_device_ids=true, to_apply=%region_4.6 | all-reduce | flops 4096 | bytes 32768 | tf_op jit(solution)/shard_map/psum | solution.py:139
  898.1 3.4 collective-permute-start.49
  901.5 2.4 collective-permute-done.49
  903.9 4.6 collective-permute-start.50
  908.5 3.1 collective-permute-done.50
  911.6 3.3 collective-permute-start.51
  914.9 3.5 collective-permute-done.51
  918.5 4.1 collective-permute-start.52
  923.3 4.9 collective-permute-done.52
  929.8 53.5 %psum.61 = f32[64,128]{1,0:T(8,128)S(1)} all-reduce(f32[64,128]{1,0:T(8,128)S(1)} %convolution_bitcast_fusion.4), channel_id=1, replica_groups=mesh['leaf'=32,'front'=16] {'front'}, use_global_device_ids=true, to_apply=%region_5.7 | all-reduce | flops 8192 | bytes 65536 | tf_op jit(solution)/shard_map/psum | solution.py:139
  986.4 3.4 collective-permute-start.54
  989.8 2.8 collective-permute-done.54
  992.6 4.6 collective-permute-start.55
  997.2 3.8 collective-permute-done.55
  1001.0 3.4 collective-permute-start.56
  1005.3 4.0 collective-permute-done.56
  1011.6 129.0 %all-reduce.15.cloned.1.call-done = f32[128,128]{0,1:T(8,128)} async-done(((f32[128,128]{0,1:T(8,128)}), f32[128,128]{0,1:T(8,128)}) %all-reduce.15.cloned.1.call-update) | async-done | bytes 65552 | tf_op jit(solution)/shard_map/psum | solution.py:139
  1144.8 3.4 collective-permute-start.58
  1149.0 3.2 collective-permute-done.58
  1152.3 4.9 collective-permute-start.59
  1158.8 4.4 collective-permute-done.59
  1167.4 128.6 %all-reduce.17.cloned.1.call-done = f32[256,128]{0,1:T(8,128)} async-done(((f32[256,128]{0,1:T(8,128)}), f32[256,128]{0,1:T(8,128)}) %all-reduce.17.cloned.1.call-update) | async-done | bytes 131088 | tf_op jit(solution)/shard_map/psum | solution.py:139
  (223 shorter events, 86.3 us)
Async XLA Ops:
  7.2 142.3 %all-reduce.7.cloned.1.call-start = ((), (), s32[]{:S(2)}) async-start(), calls=%async_computation | async-start | bytes 1048576 | tf_op jit(solution)/shard_map/psum | solution.py:34
  10.2 372.3 %all-reduce.9.cloned.1.call-start = ((), (), s32[]{:S(2)}) async-start(), calls=%async_computation.1 | async-start | bytes 524288 | tf_op jit(solution)/shard_map/psum | solution.py:34
  150.2 7.3 collective-permute-start
  157.5 7.8 collective-permute-start.1
  165.4 7.1 collective-permute-start.2
  167.3 7.1 collective-permute-start.9
  172.4 7.1 collective-permute-start.3
  174.4 7.1 collective-permute-start.10
  179.5 7.1 collective-permute-start.4
  181.5 7.9 collective-permute-start.11
  186.6 7.9 collective-permute-start.5
  189.4 7.1 collective-permute-start.12
  194.6 7.1 collective-permute-start.6
  196.6 40.6 %collective-permute-start.13 = (f32[64,128]{1,0:T(8,128)S(1)}, f32[64,128]{1,0:T(8,128)S(1)}, u32[]{:S(2)}, u32[]{:S(2)}) collective-permute-start(f32[64,128]{1,0:T(8,128)S(1)} %collective-permute-done.12), channel_id=1, source_target_pairs={{0,15},{1,0},{2,1},{3,2},{4,3},{5,4},{6,5},{7,6},{8,7},{9,8},{10,9... | collective-permute-start | bytes 98312 | tf_op jit(solution)/shard_map/ppermute | solution.py:17
  201.7 37.4 %collective-permute-start.7 = (f32[64,128]{1,0:T(8,128)S(1)}, f32[64,128]{1,0:T(8,128)S(1)}, u32[]{:S(2)}, u32[]{:S(2)}) collective-permute-start(f32[64,128]{1,0:T(8,128)S(1)} %collective-permute-done.6), channel_id=1, source_target_pairs={{0,1},{1,2},{2,3},{3,4},{4,5},{5,6},{6,7},{7,8},{8,9},{9,10},{10,1... | collective-permute-start | bytes 98312 | tf_op jit(solution)/shard_map/ppermute | solution.py:15
  237.2 6.8 collective-permute-start.14
  239.1 8.0 collective-permute-start.8
  244.0 5.8 collective-permute-start.15
  253.0 358.4 %all-reduce.11.cloned.1.call-start = ((), (), s32[]{:S(2)}) async-start(), calls=%async_computation.2 | async-start | bytes 262144 | tf_op jit(solution)/shard_map/psum | solution.py:34
  383.2 5.8 collective-permute-start.16
  389.0 7.8 collective-permute-start.17
  396.9 7.1 collective-permute-start.18
  398.8 7.1 collective-permute-start.25
  403.9 7.1 collective-permute-start.19
  405.9 7.1 collective-permute-start.26
  411.0 7.1 collective-permute-start.20
  413.0 7.1 collective-permute-start.27
  418.1 7.1 collective-permute-start.21
  420.1 7.1 collective-permute-start.28
  425.2 7.1 collective-permute-start.22
  427.2 40.3 %collective-permute-start.29 = (f32[64,128]{1,0:T(8,128)S(1)}, f32[64,128]{1,0:T(8,128)S(1)}, u32[]{:S(2)}, u32[]{:S(2)}) collective-permute-start(f32[64,128]{1,0:T(8,128)S(1)} %collective-permute-done.28), channel_id=1, source_target_pairs={{0,15},{1,0},{2,1},{3,2},{4,3},{5,4},{6,5},{7,6},{8,7},{9,8},{10,9... | collective-permute-start | bytes 98312 | tf_op jit(solution)/shard_map/ppermute | solution.py:17
  432.3 37.1 %collective-permute-start.23 = (f32[64,128]{1,0:T(8,128)S(1)}, f32[64,128]{1,0:T(8,128)S(1)}, u32[]{:S(2)}, u32[]{:S(2)}) collective-permute-start(f32[64,128]{1,0:T(8,128)S(1)} %collective-permute-done.22), channel_id=1, source_target_pairs={{0,1},{1,2},{2,3},{3,4},{4,5},{5,6},{6,7},{7,8},{8,9},{9,10},{10,1... | collective-permute-start | bytes 98312 | tf_op jit(solution)/shard_map/ppermute | solution.py:15
  467.5 6.8 collective-permute-start.30
  469.4 8.0 collective-permute-start.24
  474.2 5.8 collective-permute-start.31
  483.2 354.1 %all-reduce.13.cloned.1.call-start = ((), (), s32[]{:S(2)}) async-start(), calls=%async_computation.3 | async-start | bytes 131072 | tf_op jit(solution)/shard_map/psum | solution.py:34
  612.2 7.3 collective-permute-start.32
  619.5 7.8 collective-permute-start.33
  627.3 7.1 collective-permute-start.34
  629.2 7.1 collective-permute-start.41
  634.4 7.1 collective-permute-start.35
  636.3 7.1 collective-permute-start.42
  641.5 7.1 collective-permute-start.36
  643.4 7.1 collective-permute-start.43
  648.6 7.1 collective-permute-start.37
  650.5 7.1 collective-permute-start.44
  655.6 7.1 collective-permute-start.38
  657.6 40.3 %collective-permute-start.45 = (f32[64,128]{1,0:T(8,128)S(1)}, f32[64,128]{1,0:T(8,128)S(1)}, u32[]{:S(2)}, u32[]{:S(2)}) collective-permute-start(f32[64,128]{1,0:T(8,128)S(1)} %collective-permute-done.44), channel_id=1, source_target_pairs={{0,15},{1,0},{2,1},{3,2},{4,3},{5,4},{6,5},{7,6},{8,7},{9,8},{10,9... | collective-permute-start | bytes 98312 | tf_op jit(solution)/shard_map/ppermute | solution.py:17
  662.8 37.1 %collective-permute-start.39 = (f32[64,128]{1,0:T(8,128)S(1)}, f32[64,128]{1,0:T(8,128)S(1)}, u32[]{:S(2)}, u32[]{:S(2)}) collective-permute-start(f32[64,128]{1,0:T(8,128)S(1)} %collective-permute-done.38), channel_id=1, source_target_pairs={{0,1},{1,2},{2,3},{3,4},{4,5},{5,6},{6,7},{7,8},{8,9},{9,10},{10,1... | collective-permute-start | bytes 98312 | tf_op jit(solution)/shard_map/ppermute | solution.py:15
  697.9 6.8 collective-permute-start.46
  699.8 8.0 collective-permute-start.40
  704.7 5.8 collective-permute-start.47
  713.5 427.0 %all-reduce.15.cloned.1.call-start = ((), (), s32[]{:S(2)}) async-start(), calls=%async_computation.4 | async-start | bytes 131072 | tf_op jit(solution)/shard_map/psum | solution.py:139
  898.1 5.8 collective-permute-start.49
  903.9 7.7 collective-permute-start.50
  911.6 6.9 collective-permute-start.51
  918.5 9.8 collective-permute-start.52
  986.4 6.2 collective-permute-start.54
  992.6 8.4 collective-permute-start.55
  1001.0 8.3 collective-permute-start.56
  1011.5 284.5 %all-reduce.17.cloned.1.call-start = ((), (), s32[]{:S(2)}) async-start(), calls=%async_computation.5 | async-start | bytes 262144 | tf_op jit(solution)/shard_map/psum | solution.py:139
  1140.5 3.3 collective-permute-start.57
  1144.8 7.5 collective-permute-start.58
  1152.3 10.9 collective-permute-start.59
  (12 other events, 23.5 us)
Sparse Core Ops, SparseCore 0:
  11.2 138.1 all-reduce.6
  253.1 129.3 all-reduce.8
  483.3 128.0 all-reduce.10
  713.6 123.5 all-reduce.12
  1011.6 128.8 all-reduce.14
  1166.0 130.0 all-reduce.16
